TPU v7x, 32 devices: a whole 2x2x4 slice. The times are simulated.
32 devices in a mesh: groups: 2 (over y), row: 4 (over z), col: 4 (over x, core).
Axes of the slice: x: 2, y: 2, z: 4, core: 2. Of those that a mesh axis runs over, the one named last changes fastest.
Arguments:
- row_points: bfloat16 [32768, 512], P(('groups', 'row', 'col')), parts along dimension 0, may hold values from -8 to 8
- next_points: bfloat16 [8192, 512], P(('groups', 'row', 'col')), parts along dimension 0, may hold values from -8 to 8
- ratio: float32 [8192, 128], P(('groups', 'row', 'col')), parts along dimension 0, may hold values from 0.25 to 4
- behave_prob: float32 [8192], P(('groups', 'row', 'col')), parts along dimension 0, may hold values from 0.2 to 1
- logged_action: int32 [8192], P(('groups', 'row', 'col')), parts along dimension 0, may hold values from 0 to 3
- bucket: int32 [8192], P(('groups', 'row', 'col')), parts along dimension 0, may hold values from 0 to 63
- regime_table: int32 [128, 64], replicated, may hold values from 0 to 3
Outputs:
- proof: float32 [32768, 128], P(('groups', 'row', 'col')), parts along dimension 0
There are 2 independent parts, one for each index of `groups`. A program takes and returns all parts, laid end to end along the dimension named above; an argument that names none is the same for every part. Nothing has to cross between parts.
All inputs are finite; a program needn't handle non-finite values.
Results may differ from a plain program's by a relative error of at most 0.0028.
Values may be sent and summed in bfloat16 or wider, within the bound.
A program may use at most 64 MiB of HBM per device.

v0:
```python
import math

import jax
import jax.numpy as jnp
from jax import lax
from jax.sharding import PartitionSpec as P

BUCKETS = 64
STEPS = 4


KERNEL_SCALE = 0.5
DISCOUNT = 0.9


def passed_along(block, axis, distance):
    devices = range(lax.axis_size(axis))
    route = [((i - distance) % len(devices), i) for i in devices]
    return lax.ppermute(block, axis, route)


def residual_block(ratio, behave_prob, logged_action, bucket, regime_table):
    onehot = (bucket[:, None] == jnp.arange(BUCKETS, dtype=jnp.int32)[None, :]).astype(jnp.float32)
    chosen = jnp.dot(onehot, regime_table.astype(jnp.float32).T, precision=lax.Precision.HIGHEST)
    matched = (chosen == logged_action.astype(jnp.float32)[:, None]).astype(jnp.float32)
    importance = matched / behave_prob[:, None]
    return ((DISCOUNT * importance - 1.0) * ratio).astype(jnp.bfloat16)


def kernel_tile(row_block, row_norm, column_block):
    features = row_block.shape[1]
    columns = column_block[:, :features]
    residual = column_block[:, features:]
    column_norm = jnp.sum(jnp.square(columns.astype(jnp.float32)), axis=1)
    inner_terms = lax.dot_general(
        row_block, columns, (((1,), (1,)), ((), ())), preferred_element_type=jnp.float32
    )
    coefficient = KERNEL_SCALE / math.sqrt(features)
    exponent = coefficient * (
        2.0 * inner_terms - row_norm[:, None] - column_norm[None, :] + 2.0 * features
    )
    kernel = jnp.exp(exponent).astype(jnp.bfloat16)
    return jnp.dot(kernel, residual, preferred_element_type=jnp.float32)


def body(row_points, next_points, ratio, behave_prob, logged_action, bucket, regime_table):
    residual = residual_block(ratio, behave_prob, logged_action, bucket, regime_table)
    packed = jnp.concatenate([next_points, residual], axis=1)
    row_norm = jnp.sum(jnp.square(row_points.astype(jnp.float32)), axis=1)
    col_count = lax.axis_size("col")
    local_rows = next_points.shape[0]
    summed = jnp.zeros((row_points.shape[0], ratio.shape[1]), jnp.float32)
    pieces = [packed]
    for offset in range(1, STEPS):
        pieces.append(passed_along(packed, "row", -offset))
    stacked = jnp.stack(pieces, axis=0)
    gathered = lax.all_gather(stacked, "col", axis=1, tiled=True)
    for section in range(STEPS):
        summed = summed + kernel_tile(row_points, row_norm, gathered[section])
    return summed / float(STEPS * col_count * local_rows)


def solution(mesh):
    placed = (
        P(("groups", "row", "col"), None),
        P(("groups", "row", "col"), None),
        P(("groups", "row", "col"), None),
        P(("groups", "row", "col")),
        P(("groups", "row", "col")),
        P(("groups", "row", "col")),
        P(),
    )
    return jax.shard_map(
        body,
        mesh=mesh,
        in_specs=placed,
        out_specs=P(("groups", "row", "col"), None),
        check_vma=False,
    )
```

profile of v0, /device:TPU:0, one launch (start us, length us, event | category | flops | bytes accessed | tf_op | source)
XLA Modules:
  0.0 115.2 jit_solution(2925726039710852896)
XLA Ops:
  6.5 0.0 all-gather.2.cloned.1.call-start
  6.5 1.0 copy.8
  7.5 0.7 convert_element_type.41
  8.2 1.1 fusion.7
  9.3 0.1 copy.9
  9.4 1.0 fusion.34
  10.4 0.0 copy-start.2
  10.4 5.1 %collective-permute-start = (bf16[256,640]{1,0:T(8,128)(2,1)S(1)}, bf16[256,640]{1,0:T(8,128)(2,1)S(1)}, u32[]{:S(2)}, u32[]{:S(2)}) collective-permute-start(bf16[256,640]{1,0:T(8,128)(2,1)S(1)} %get-tuple-element.10), channel_id=1, source_target_pairs={{4,0},{8,4},{12,8},{0,12},{5,1},{9,5},{13,9},{1,13},{6,2},{10,6},{... | collective-permute-start | bytes 983048 | tf_op jit(solution)/shard_map/ppermute | solution.py:19
  15.5 0.0 collective-permute-start.1
  15.6 1.0 collective-permute-start.2
  16.6 7.1 %collective-permute-done = bf16[256,640]{1,0:T(8,128)(2,1)S(1)} collective-permute-done((bf16[256,640]{1,0:T(8,128)(2,1)S(1)}, bf16[256,640]{1,0:T(8,128)(2,1)S(1)}, u32[]{:S(2)}, u32[]{:S(2)}) %collective-permute-start) | collective-permute-done | bytes 327712 | tf_op jit(solution)/shard_map/ppermute | solution.py:19
  23.7 19.8 %collective-permute-done.1 = bf16[256,640]{1,0:T(8,128)(2,1)S(1)} collective-permute-done((bf16[256,640]{1,0:T(8,128)(2,1)S(1)}, bf16[256,640]{1,0:T(8,128)(2,1)S(1)}, u32[]{:S(2)}, u32[]{:S(2)}) %collective-permute-start.1) | collective-permute-done | bytes 327712 | tf_op jit(solution)/shard_map/ppermute | solution.py:19
  43.5 0.0 collective-permute-done.2
  43.5 1.3 %pad_maximum_fusion = bf16[4,256,640]{2,1,0:T(8,128)(2,1)} fusion(bf16[1,256,640]{2,1,0:T(8,128)(2,1)S(1)} %bitcast.19, bf16[1,256,640]{2,1,0:T(8,128)(2,1)S(1)} %bitcast.18, bf16[1,256,640]{2,1,0:T(8,128)(2,1)S(1)} %bitcast.17, bf16[1,256,640]{2,1,0:T(8,128)(2,1)S(1)} %get-tuple-element.9), kind=kLoop, calls=%fused_computation.13 | loop fusion | flops 1966080 | bytes 2621440 | tf_op jit(solution)/shard_map/stack | solution.py:56
  44.8 0.0 all-gather.2.cloned.1.call-update
  44.8 0.0 copy-done.2
  44.8 0.3 multiply_reduce_fusion.4
  45.1 40.7 %all-gather.2.cloned.1.call-done = bf16[4,1024,640]{2,1,0:T(8,128)(2,1)} async-done(((bf16[4,256,640]{2,1,0:T(8,128)(2,1)}), bf16[4,1024,640]{2,1,0:T(8,128)(2,1)}) %all-gather.2.cloned.1.call-update) | async-done | bytes 5242896 | tf_op jit(solution)/shard_map/all_gather | solution.py:57
  85.8 3.0 %slice_bitcast_fusion = (bf16[1024,640]{1,0:T(8,128)(2,1)S(1)}, bf16[1024,640]{1,0:T(8,128)(2,1)S(1)}, bf16[1024,640]{1,0:T(8,128)(2,1)S(1)}, bf16[1024,640]{1,0:T(8,128)(2,1)S(1)}) fusion(bf16[4,1024,640]{2,1,0:T(8,128)(2,1)} %all-gather.2.cloned.1.call-done), kind=kLoop, calls=%fused_computation.9 | loop fusion | bytes 10485760 | tf_op jit(solution)/shard_map/squeeze | solution.py:59
  88.8 0.0 copy-start
  88.8 0.0 copy-start.1
  88.8 1.0 copy-done
  89.9 0.5 multiply_reduce_fusion.2
  90.3 0.0 copy-done.1
  90.3 5.2 %fusion.1 = f32[1024,128]{1,0:T(8,128)} fusion(bf16[1024,512]{1,0:T(8,128)(2,1)} %param.7, f32[1024]{0:T(1024)S(1)} %get-tuple-element.14, f32[1024]{0:T(1024)S(1)} %multiply_reduce_fusion.4, bf16[1024,640]{1,0:T(8,128)(2,1)} %copy-done.1), kind=kOutput, calls=%fused_computation.18 | convolution fusion | flops 1348468736 | bytes 2891776 | tf_op jit(solution)/shard_map/dot_general | solution.py:43
  95.5 3.9 %convolution_add_fusion.2 = f32[1024,128]{1,0:T(8,128)S(1)} fusion(f32[1024,128]{1,0:T(8,128)} %fusion.1, bf16[1024,512]{1,0:T(8,128)(2,1)} %param.7, f32[1024]{0:T(1024)S(1)} %get-tuple-element.13, f32[1024]{0:T(1024)S(1)} %multiply_reduce_fusion.4, bf16[1024,640]{1,0:T(8,128)(2,1)} %copy-done), kind=kOutput, calls=%fused_computation.17 | convolution fusion | flops 1348599808 | bytes 3416064 | tf_op jit(solution)/shard_map/dot_general | solution.py:43
  99.4 0.5 multiply_reduce_fusion
  99.9 4.1 %convolution_add_fusion.1 = f32[1024,128]{1,0:T(8,128)} fusion(f32[1024,128]{1,0:T(8,128)S(1)} %convolution_add_fusion.2, bf16[1024,512]{1,0:T(8,128)(2,1)} %param.7, f32[1024]{0:T(1024)S(1)} %get-tuple-element.12, f32[1024]{0:T(1024)S(1)} %multiply_reduce_fusion.4, bf16[1024,640]{1,0:T(8,128)(2,1)S(1)} %get-tuple-element.6), kind=kOutput, calls=%fused_computation.16 | convolution fusion | flops 1348599808 | bytes 3416064 | tf_op jit(solution)/shard_map/dot_general | solution.py:43
  104.0 4.3 %fusion = f32[1024,128]{1,0:T(8,128)} fusion(f32[1024,128]{1,0:T(8,128)} %convolution_add_fusion.1, bf16[1024,512]{1,0:T(8,128)(2,1)} %param.7, f32[1024]{0:T(1024)S(1)} %get-tuple-element.11, f32[1024]{0:T(1024)S(1)} %multiply_reduce_fusion.4, bf16[1024,640]{1,0:T(8,128)(2,1)S(1)} %get-tuple-element.5), kind=kOutput, calls=%fused_computation.15 | convolution fusion | flops 1348730880 | bytes 3416064 | tf_op jit(solution)/shard_map/dot_general | solution.py:43
Async XLA Ops:
  6.5 79.3 %all-gather.2.cloned.1.call-start = ((), (), s32[]{:S(2)}) async-start(), calls=%async_computation | async-start | bytes 6553600 | tf_op jit(solution)/shard_map/all_gather | solution.py:57
  10.4 34.4 %copy-start.2 = (bf16[1024,512]{1,0:T(8,128)(2,1)S(1)}, bf16[1024,512]{1,0:T(8,128)(2,1)}, u32[]{:S(2)}) copy-start(bf16[1024,512]{1,0:T(8,128)(2,1)} %param.7) | copy-start | bytes 3145732
  10.4 13.3 %collective-permute-start = (bf16[256,640]{1,0:T(8,128)(2,1)S(1)}, bf16[256,640]{1,0:T(8,128)(2,1)S(1)}, u32[]{:S(2)}, u32[]{:S(2)}) collective-permute-start(bf16[256,640]{1,0:T(8,128)(2,1)S(1)} %get-tuple-element.10), channel_id=1, source_target_pairs={{4,0},{8,4},{12,8},{0,12},{5,1},{9,5},{13,9},{1,13},{6,2},{10,6},{... | collective-permute-start | bytes 983048 | tf_op jit(solution)/shard_map/ppermute | solution.py:19
  15.5 27.9 %collective-permute-start.1 = (bf16[256,640]{1,0:T(8,128)(2,1)S(1)}, bf16[256,640]{1,0:T(8,128)(2,1)S(1)}, u32[]{:S(2)}, u32[]{:S(2)}) collective-permute-start(bf16[256,640]{1,0:T(8,128)(2,1)S(1)} %get-tuple-element.10), channel_id=1, source_target_pairs={{8,0},{12,4},{0,8},{4,12},{9,1},{13,5},{1,9},{5,13},{10,2},{14,6},... | collective-permute-start | bytes 983048 | tf_op jit(solution)/shard_map/ppermute | solution.py:19
  15.6 27.9 %collective-permute-start.2 = (bf16[256,640]{1,0:T(8,128)(2,1)S(1)}, bf16[256,640]{1,0:T(8,128)(2,1)S(1)}, u32[]{:S(2)}, u32[]{:S(2)}) collective-permute-start(bf16[256,640]{1,0:T(8,128)(2,1)S(1)} %get-tuple-element.10), channel_id=1, source_target_pairs={{12,0},{0,4},{4,8},{8,12},{13,1},{1,5},{5,9},{9,13},{14,2},{2,6},{... | collective-permute-start | bytes 983048 | tf_op jit(solution)/shard_map/ppermute | solution.py:19
  88.8 1.1 copy-start
  88.8 1.5 %copy-start.1 = (bf16[1024,640]{1,0:T(8,128)(2,1)}, bf16[1024,640]{1,0:T(8,128)(2,1)S(1)}, u32[]{:S(2)}) copy-start(bf16[1024,640]{1,0:T(8,128)(2,1)S(1)} %get-tuple-element.8) | copy-start | bytes 3932164
Sparse Core Ops, SparseCore 0:
  44.9 40.8 all-gather.1
where the time goes:
time: 116 us; the launch traced here: 115 us
  waiting for transfers between devices  67.7 us (58%)
  matrix products  18.6 us (16%)
  between operations  13.5 us (12%)
  starting transfers between devices  6.12 us (5%)
  local copies, waits for them, and re-layouts  5.11 us (4%)
  other arithmetic  4.22 us (4%)
    all_gather x1, waiting for transfers between devices, body(): gathered = lax.all_gather(stacked, 'col', axis=1, tiled=True)  40.7 us
    ppermute x3, waiting for transfers between devices, passed_along(): return lax.ppermute(block, axis, route)  26.9 us
    dot_general x4, matrix products, kernel_tile(): return jnp.dot(kernel, residual, preferred_element_type=jnp.float32)  17.5 us
    ppermute x3, starting transfers between devices, passed_along(): return lax.ppermute(block, axis, route)  6.11 us
    squeeze x1, local copies, waits for them, and re-layouts, body(): summed = summed + kernel_tile(row_points, row_norm, gathered[section])  2.95 us
  transfers between devices with their start and end apart: 4, of which 3 were waited for; matrix products, arithmetic and copies ran while one was open for 0% of the time, Pallas kernels for 0%

commit v1 on v0

--- a/solution.py
+++ b/solution.py
@@ -1,8 +1,11 @@
+import functools
 import math
 
 import jax
 import jax.numpy as jnp
 from jax import lax
+from jax.experimental import pallas as pl
+from jax.experimental.pallas import tpu as pltpu
 from jax.sharding import PartitionSpec as P
 
 BUCKETS = 64
@@ -43,7 +46,7 @@
     return jnp.dot(kernel, residual, preferred_element_type=jnp.float32)
 
 
-def body(row_points, next_points, ratio, behave_prob, logged_action, bucket, regime_table):
+def gathered_body(row_points, next_points, ratio, behave_prob, logged_action, bucket, regime_table):
     residual = residual_block(ratio, behave_prob, logged_action, bucket, regime_table)
     packed = jnp.concatenate([next_points, residual], axis=1)
     row_norm = jnp.sum(jnp.square(row_points.astype(jnp.float32)), axis=1)
@@ -60,7 +63,266 @@
     return summed / float(STEPS * col_count * local_rows)
 
 
+SUBS = 2
+PARTNER, ACROSS, BESIDE, SIBLING = range(4)
+
+
+def interleaved(*lists):
+    merged = []
+    for order, entries in enumerate(lists):
+        merged += [(place, order, entry) for place, entry in enumerate(entries)]
+    return [entry for _, _, entry in sorted(merged, key=lambda item: item[:2])]
+
+
+def arrivals(subs):
+    half = subs // 2
+    every = list(range(subs))
+
+    def block(other_column, end, other_side, parts, *directions):
+        return [(other_column, end, other_side, part, directions + (SIBLING,)) for part in parts]
+
+    at_end = interleaved(
+        block(0, 0, 0, every[:half], BESIDE)
+        + block(0, 0, 0, every[half:])
+        + block(0, 0, 1, every, BESIDE)
+        + block(0, 1, 1, every, BESIDE)
+        + block(1, 0, 0, every[half:]),
+        block(1, 1, 0, every, PARTNER)
+        + block(1, 0, 0, every[:half])
+        + block(1, 0, 1, every)
+        + block(1, 1, 1, every),
+    )
+    at_middle = interleaved(
+        block(0, 0, 1, every, PARTNER, BESIDE) + block(0, 1, 1, every, PARTNER, BESIDE),
+        block(0, 1, 0, every, ACROSS) + block(1, 1, 0, every),
+        block(1, 0, 0, every[half:], PARTNER)
+        + block(1, 0, 0, every[:half])
+        + block(1, 0, 1, every)
+        + block(1, 1, 1, every),
+    )
+    return at_end, at_middle
+
+
+def proof_kernel(
+    scale, rows_ref, next_ref, ratio_ref, behave_ref, action_ref, bucket_ref, table_ref, out_ref,
+    held, row_term, send_sem, recv_sem,
+):
+    z, col = lax.axis_index("row"), lax.axis_index("col")
+    x, core = col // 2, col % 2
+    is_end = (z == 0) | (z == 3)
+    is_middle = jnp.logical_not(is_end)
+    side = z // 2
+    shard, features = next_ref.shape
+    sub_rows = shard // SUBS
+    width = 2 * sub_rows
+    partner = z + 1 - 2 * (z % 2)
+    target = {
+        PARTNER: (partner, col),
+        ACROSS: (3 - z, col),
+        BESIDE: (z, (1 - x) * 2 + core),
+        SIBLING: (z, x * 2 + 1 - core),
+    }
+
+    def device(direction):
+        to_row, to_col = target[direction]
+        return {"row": to_row, "col": to_col}
+
+    def unit_of(other_column, end, other_side, sub):
+        bx = (1 - x) if other_column else x
+        bside = (1 - side) if other_side else side
+        bz = 3 * bside if end else 1 + bside
+        return (bx * 4 + bz) * SUBS + sub
+
+    def part(unit, of_core):
+        return held.at[pl.ds(pl.multiple_of((unit * 2 + of_core) * sub_rows, sub_rows), sub_rows), :]
+
+    def transfer(unit, of_core, direction):
+        return pltpu.make_async_remote_copy(
+            src_ref=part(unit, of_core),
+            dst_ref=part(unit, of_core),
+            send_sem=send_sem.at[unit, direction],
+            recv_sem=recv_sem.at[unit * 2 + of_core],
+            device_id=device(direction),
+            device_id_type=pl.DeviceIdType.MESH,
+        )
+
+    barrier = pltpu.get_barrier_semaphore()
+
+    def greet(direction):
+        pl.semaphore_signal(
+            barrier, inc=1, device_id=device(direction), device_id_type=pl.DeviceIdType.MESH
+        )
+
+    greet(PARTNER)
+    greet(BESIDE)
+    greet(SIBLING)
+
+    @pl.when(is_middle)
+    def _():
+        greet(ACROSS)
+
+    mine = (x * 4 + z) * SUBS
+    columns = jnp.concatenate(
+        [
+            bucket_ref[...].astype(jnp.float32),
+            action_ref[...].astype(jnp.float32),
+            behave_ref[...],
+            jnp.zeros((5, shard), jnp.float32),
+        ],
+        axis=0,
+    ).T
+    buckets = table_ref.shape[1]
+    onehot = (columns[:, 0:1] == lax.broadcasted_iota(jnp.int32, (shard, buckets), 1).astype(jnp.float32))
+    chosen = lax.dot_general(
+        onehot.astype(jnp.float32).astype(jnp.bfloat16),
+        table_ref[...].astype(jnp.float32).astype(jnp.bfloat16),
+        (((1,), (1,)), ((), ())),
+        preferred_element_type=jnp.float32,
+    )
+    matched = jnp.where(chosen == columns[:, 1:2], 1.0, 0.0)
+    importance = matched / columns[:, 2:3]
+    residual = ((DISCOUNT * importance - 1.0) * ratio_ref[...]).astype(jnp.bfloat16)
+    for sub in range(SUBS):
+        own = part(mine + sub, core)
+        own[:, :features] = next_ref[sub * sub_rows:(sub + 1) * sub_rows, :]
+        own[:, features:] = residual[sub * sub_rows:(sub + 1) * sub_rows, :]
+
+    pl.semaphore_wait(barrier, jnp.where(is_end, 3, 4))
+
+    half = SUBS // 2
+    for sub in range(SUBS):
+        for direction in (PARTNER, SIBLING):
+            transfer(mine + sub, core, direction).start()
+
+        @pl.when(is_end)
+        def _():
+            transfer(mine + sub, core, BESIDE).start()
+
+        @pl.when(is_middle)
+        def _():
+            transfer(mine + sub, core, ACROSS).start()
+            transfer(mine + (sub + half) % SUBS, core, BESIDE).start()
+
+    fold = KERNEL_SCALE / math.sqrt(features) * math.log2(math.e)
+    row_count = rows_ref.shape[0]
+    tile = min(256, row_count)
+
+    @pl.loop(0, row_count // tile)
+    def _(step):
+        here = pl.ds(pl.multiple_of(step * tile, tile), tile)
+        squares = jnp.square(rows_ref[here, :].astype(jnp.float32))
+        row_term[here, :] = fold * (2.0 * features - jnp.sum(squares, axis=1, keepdims=True))
+        out_ref[here, :] = jnp.zeros((tile, out_ref.shape[1]), jnp.float32)
+
+    def add_unit(unit):
+        start = pl.ds(pl.multiple_of(unit * width, width), width)
+        points = held[start, :features]
+        weights = held[start, features:]
+        squares = jnp.square(points.astype(jnp.float32))
+        high = squares.astype(jnp.bfloat16)
+        low = (squares - high.astype(jnp.float32)).astype(jnp.bfloat16)
+        ones = jnp.ones((16, features), jnp.bfloat16)
+        contract = (((1,), (1,)), ((), ()))
+        norm = lax.dot_general(ones, high, contract, preferred_element_type=jnp.float32)
+        norm += lax.dot_general(ones, low, contract, preferred_element_type=jnp.float32)
+        column_term = fold * norm[0:1, :]
+
+        @pl.loop(0, row_count // tile)
+        def _(step):
+            here = pl.ds(pl.multiple_of(step * tile, tile), tile)
+            inner = lax.dot_general(
+                rows_ref[here, :], points, contract, preferred_element_type=jnp.float32
+            )
+            exponent = (2.0 * fold) * inner + (row_term[here, :] - column_term)
+            kernel = jnp.exp2(exponent).astype(jnp.bfloat16)
+            out_ref[here, :] += jnp.dot(kernel, weights, preferred_element_type=jnp.float32)
+
+    waiting = [mine + sub for sub in range(SUBS)]
+
+    def add_oldest():
+        unit = waiting.pop(0)
+        transfer(unit, 1 - core, SIBLING).wait_recv()
+        add_unit(unit)
+
+    at_end, at_middle = arrivals(SUBS)
+    passed = []
+    for end_entry, middle_entry in zip(at_end, at_middle, strict=True):
+        unit = jnp.where(is_end, unit_of(*end_entry[:4]), unit_of(*middle_entry[:4]))
+        transfer(unit, core, SIBLING).wait_recv()
+        for direction in (BESIDE, PARTNER, ACROSS, SIBLING):
+            in_end, in_middle = direction in end_entry[4], direction in middle_entry[4]
+            if in_end and in_middle:
+                transfer(unit, core, direction).start()
+            elif in_end or in_middle:
+
+                @pl.when(is_end if in_end else is_middle)
+                def _():
+                    transfer(unit, core, direction).start()
+
+            passed.append((unit, direction, in_end, in_middle))
+        waiting.append(unit)
+        if len(waiting) > 1:
+            add_oldest()
+    while waiting:
+        add_oldest()
+
+    @pl.loop(0, row_count // tile)
+    def _(step):
+        here = pl.ds(pl.multiple_of(step * tile, tile), tile)
+        out_ref[here, :] = out_ref[here, :] / scale
+
+    for sub in range(SUBS):
+        for direction in (PARTNER, BESIDE, SIBLING):
+            transfer(mine + sub, core, direction).wait_send()
+
+        @pl.when(is_middle)
+        def _():
+            transfer(mine + sub, core, ACROSS).wait_send()
+
+    for unit, direction, in_end, in_middle in passed:
+        if in_end and in_middle:
+            transfer(unit, core, direction).wait_send()
+        elif in_end or in_middle:
+
+            @pl.when(is_end if in_end else is_middle)
+            def _():
+                transfer(unit, core, direction).wait_send()
+
+
+def relayed_body(row_points, next_points, ratio, behave_prob, logged_action, bucket, regime_table):
+    rows, features = row_points.shape
+    shard, regimes = ratio.shape
+    devices = lax.axis_size("row") * lax.axis_size("col")
+    columns = devices * shard
+    units = devices // 2 * SUBS
+    return pl.pallas_call(
+        functools.partial(proof_kernel, float(columns)),
+        out_shape=jax.ShapeDtypeStruct((rows, regimes), jnp.float32),
+        in_specs=[pl.BlockSpec(memory_space=pltpu.VMEM)] * 7,
+        out_specs=pl.BlockSpec(memory_space=pltpu.VMEM),
+        scratch_shapes=[
+            pltpu.VMEM((columns, features + regimes), jnp.bfloat16),
+            pltpu.VMEM((rows, 1), jnp.float32),
+            pltpu.SemaphoreType.DMA((units, 4)),
+            pltpu.SemaphoreType.DMA((units * 2,)),
+        ],
+        compiler_params=pltpu.CompilerParams(
+            collective_id=0, has_side_effects=True, vmem_limit_bytes=40 * 2**20
+        ),
+    )(
+        row_points,
+        next_points,
+        ratio,
+        behave_prob.reshape(1, shard),
+        logged_action.reshape(1, shard),
+        bucket.reshape(1, shard),
+        regime_table,
+    )
+
+
 def solution(mesh):
+    whole_window = mesh.shape["row"] == STEPS == 4 and mesh.shape["col"] == 4
+    body = relayed_body if whole_window else gathered_body
     placed = (
         P(("groups", "row", "col"), None),
         P(("groups", "row", "col"), None),

time: 116 us -> 52.8 us (0.46)
  waiting for transfers between devices: 67.7 us -> 0 us
  Pallas kernels: 0 us -> 47.7 us
  matrix products: 18.6 us -> 0 us
  between operations: 13.5 us -> 0.05 us
  starting transfers between devices: 6.12 us -> 0 us
  other arithmetic: 4.22 us -> 0 us
    pallas_call x0 -> x1, Pallas kernels: none -> 47.7 us  [relayed_body(): pl.pallas_call(functools.partial(proof_kernel, float(columns)), out_shape...]
    all_gather x1 -> x0, waiting for transfers between devices: 40.7 us -> none  [body(): gathered = lax.all_gather(stacked, 'col', axis=1, tiled=True)]
    ppermute x3 -> x0, waiting for transfers between devices: 26.9 us -> none  [passed_along(): return lax.ppermute(block, axis, route)]
    dot_general x5 -> x0, matrix products: 18.6 us -> none  [the longest x4 17.5 us: kernel_tile(): return jnp.dot(kernel, residual, preferred_element_type=jnp.float32)]
    ppermute x3 -> x0, starting transfers between devices: 6.11 us -> none  [passed_along(): return lax.ppermute(block, axis, route)]
    squeeze x1 -> x0, local copies, waits for them, and re-layouts: 2.95 us -> none  [body(): summed = summed + kernel_tile(row_points, row_norm, gathered[section])]
    unnamed x7 -> x14, local copies, waits for them, and re-layouts: 2.05 us -> 4.77 us
    another operation x2 -> x0, other arithmetic: 2.3 us -> none  [body(): stacked = jnp.stack(pieces, axis=0)]
  transfers between devices with their start and end apart: 4 -> 0, of which waited for: 3 -> 0; matrix products, arithmetic and copies ran while one was open for 0% -> 0% of each run, Pallas kernels for 0% -> 0%
where the time goes in v1:
time: 52.8 us; the launch traced here: 52.5 us
  Pallas kernels  47.7 us (90%)
  local copies, waits for them, and re-layouts  4.77 us (9%)
    pallas_call x1, Pallas kernels, relayed_body(): pl.pallas_call(functools.partial(proof_kernel, float(columns)), out_shape...  47.7 us
    unnamed x14, local copies, waits for them, and re-layouts  4.77 us

profile of v1, /device:TPU:0, one launch (start us, length us, event | category | flops | bytes accessed | tf_op | source)
XLA Modules:
  0.0 52.5 jit_solution(16347028945505257517)
XLA Ops:
  0.0 0.0 copy-start.3
  0.0 0.0 copy-start.4
  0.0 0.0 copy-start.5
  0.0 0.9 %copy.8.table_ref = s32[128,64]{1,0:T(8,128)S(1)} copy(s32[128,64]{0,1:T(8,128)} %param.13) | data formatting | bytes 65536 | tf_op args[6]
  0.9 0.0 copy-done.3
  0.9 0.0 copy-done.4
  0.9 0.0 copy-done.5
  0.9 0.0 copy-start
  0.9 1.2 %copy-done = bf16[1024,512]{1,0:T(8,128)(2,1)S(1)} copy-done((bf16[1024,512]{1,0:T(8,128)(2,1)S(1)}, bf16[1024,512]{1,0:T(8,128)(2,1)}, u32[]{:S(2)}) %copy-start) | copy-done | bytes 1048600
  2.2 0.0 copy-start.1
  2.2 0.9 %copy-done.1 = bf16[256,512]{1,0:T(8,128)(2,1)S(1)} copy-done((bf16[256,512]{1,0:T(8,128)(2,1)S(1)}, bf16[256,512]{1,0:T(8,128)(2,1)}, u32[]{:S(2)}) %copy-start.1) | copy-done | bytes 262168
  3.1 0.0 copy-start.2
  3.1 0.9 %copy-done.2 = f32[256,128]{1,0:T(8,128)S(1)} copy-done((f32[256,128]{1,0:T(8,128)S(1)}, f32[256,128]{1,0:T(8,128)}, u32[]{:S(2)}) %copy-start.2) | copy-done | bytes 131096
  4.0 47.7 %shard_map.73 = f32[1024,128]{1,0:T(8,128)S(1)} custom-call(bf16[1024,512]{1,0:T(8,128)(2,1)S(1)} %copy-done, bf16[256,512]{1,0:T(8,128)(2,1)S(1)} %copy-done.1, f32[256,128]{1,0:T(8,128)S(1)} %copy-done.2, f32[1,256]{1,0:T(1,128)S(1)} %bitcast.3, s32[1,256]{1,0:T(1,128)S(1)} %bitcast.4, s32[1,256]{1,0:T(1,128)S(1)} %bitcast.5, s32[128,64]{1,0:T(8,128)S(1)} %copy.8.table_ref), custom_call_target="tpu_custom_call" | custom-call | tf_op jit(solution)/shard_map/pallas_call | solution.py:298
  51.7 0.8 %copy.10 = f32[1024,128]{1,0:T(8,128)} copy(f32[1024,128]{1,0:T(8,128)S(1)} %shard_map.73) | data formatting | bytes 1048576
Async XLA Ops:
  0.0 0.9 %copy-start.3 = (f32[256]{0:T(256)S(1)}, f32[256]{0:T(256)}, u32[]{:S(2)}) copy-start(f32[256]{0:T(256)} %param.10) | copy-start | bytes 3076
  0.0 0.9 %copy-start.4 = (s32[256]{0:T(256)S(1)}, s32[256]{0:T(256)}, u32[]{:S(2)}) copy-start(s32[256]{0:T(256)} %param.11) | copy-start | bytes 3076
  0.0 0.9 %copy-start.5 = (s32[256]{0:T(256)S(1)}, s32[256]{0:T(256)}, u32[]{:S(2)}) copy-start(s32[256]{0:T(256)} %param.12) | copy-start | bytes 3076
  0.9 1.2 %copy-start = (bf16[1024,512]{1,0:T(8,128)(2,1)S(1)}, bf16[1024,512]{1,0:T(8,128)(2,1)}, u32[]{:S(2)}) copy-start(bf16[1024,512]{1,0:T(8,128)(2,1)} %rows_ref.1) | copy-start | bytes 3145732
  2.2 0.9 %copy-start.1 = (bf16[256,512]{1,0:T(8,128)(2,1)S(1)}, bf16[256,512]{1,0:T(8,128)(2,1)}, u32[]{:S(2)}) copy-start(bf16[256,512]{1,0:T(8,128)(2,1)} %next_ref.1) | copy-start | bytes 786436
  3.1 0.9 %copy-start.2 = (f32[256,128]{1,0:T(8,128)S(1)}, f32[256,128]{1,0:T(8,128)}, u32[]{:S(2)}) copy-start(f32[256,128]{1,0:T(8,128)} %ratio_ref.1) | copy-start | bytes 393220

commit v2 on v1

--- a/solution.py
+++ b/solution.py
@@ -63,7 +63,7 @@
     return summed / float(STEPS * col_count * local_rows)
 
 
-SUBS = 2
+SUBS = 4
 PARTNER, ACROSS, BESIDE, SIBLING = range(4)
 
 
@@ -103,18 +103,29 @@
     return at_end, at_middle
 
 
+def complete_groups(entries, group):
+    count, found = {}, []
+    for step, (other_column, end, other_side, sub, _) in enumerate(entries):
+        key = (other_column, end, other_side, sub // group * group)
+        count[key] = count.get(key, 0) + 1
+        if count[key] == group:
+            found.append((step,) + key)
+    return found
+
+
 def proof_kernel(
-    scale, rows_ref, next_ref, ratio_ref, behave_ref, action_ref, bucket_ref, table_ref, out_ref,
-    held, row_term, send_sem, recv_sem,
+    rows_hbm, next_hbm, ratio_hbm, behave_ref, action_ref, bucket_ref, table_ref, out_ref,
+    held, rows_ref, ratio_ref, row_term, local_sem, send_sem, recv_sem,
 ):
     z, col = lax.axis_index("row"), lax.axis_index("col")
     x, core = col // 2, col % 2
     is_end = (z == 0) | (z == 3)
     is_middle = jnp.logical_not(is_end)
     side = z // 2
-    shard, features = next_ref.shape
+    shard, features = next_hbm.shape
     sub_rows = shard // SUBS
-    width = 2 * sub_rows
+    group = SUBS // 2
+    width = 2 * group * sub_rows
     partner = z + 1 - 2 * (z % 2)
     target = {
         PARTNER: (partner, col),
@@ -162,6 +173,20 @@
         greet(ACROSS)
 
     mine = (x * 4 + z) * SUBS
+    ratio_copy = pltpu.make_async_copy(ratio_hbm, ratio_ref, local_sem.at[0])
+    ratio_copy.start()
+    next_copies = []
+    for sub in range(SUBS):
+        next_copies.append(
+            pltpu.make_async_copy(
+                next_hbm.at[pl.ds(sub * sub_rows, sub_rows), :],
+                part(mine + sub, core).at[:, pl.ds(0, features)],
+                local_sem.at[2 + sub],
+            )
+        )
+        next_copies[sub].start()
+    rows_copy = pltpu.make_async_copy(rows_hbm, rows_ref, local_sem.at[1])
+    rows_copy.start()
     columns = jnp.concatenate(
         [
             bucket_ref[...].astype(jnp.float32),
@@ -171,22 +196,24 @@
         ],
         axis=0,
     ).T
-    buckets = table_ref.shape[1]
+    buckets = table_ref.shape[0]
     onehot = (columns[:, 0:1] == lax.broadcasted_iota(jnp.int32, (shard, buckets), 1).astype(jnp.float32))
     chosen = lax.dot_general(
         onehot.astype(jnp.float32).astype(jnp.bfloat16),
         table_ref[...].astype(jnp.float32).astype(jnp.bfloat16),
-        (((1,), (1,)), ((), ())),
+        (((1,), (0,)), ((), ())),
         preferred_element_type=jnp.float32,
     )
     matched = jnp.where(chosen == columns[:, 1:2], 1.0, 0.0)
     importance = matched / columns[:, 2:3]
+    ratio_copy.wait()
     residual = ((DISCOUNT * importance - 1.0) * ratio_ref[...]).astype(jnp.bfloat16)
     for sub in range(SUBS):
         own = part(mine + sub, core)
-        own[:, :features] = next_ref[sub * sub_rows:(sub + 1) * sub_rows, :]
         own[:, features:] = residual[sub * sub_rows:(sub + 1) * sub_rows, :]
 
+    for copy in next_copies:
+        copy.wait()
     pl.semaphore_wait(barrier, jnp.where(is_end, 3, 4))
 
     half = SUBS // 2
@@ -204,6 +231,7 @@
             transfer(mine + (sub + half) % SUBS, core, BESIDE).start()
 
     fold = KERNEL_SCALE / math.sqrt(features) * math.log2(math.e)
+    rows_copy.wait()
     row_count = rows_ref.shape[0]
     tile = min(256, row_count)
 
@@ -214,39 +242,32 @@
         row_term[here, :] = fold * (2.0 * features - jnp.sum(squares, axis=1, keepdims=True))
         out_ref[here, :] = jnp.zeros((tile, out_ref.shape[1]), jnp.float32)
 
-    def add_unit(unit):
-        start = pl.ds(pl.multiple_of(unit * width, width), width)
+    def add_group(unit):
+        start = pl.ds(pl.multiple_of(unit * 2 * sub_rows, width), width)
         points = held[start, :features]
         weights = held[start, features:]
         squares = jnp.square(points.astype(jnp.float32))
-        high = squares.astype(jnp.bfloat16)
-        low = (squares - high.astype(jnp.float32)).astype(jnp.bfloat16)
-        ones = jnp.ones((16, features), jnp.bfloat16)
-        contract = (((1,), (1,)), ((), ()))
-        norm = lax.dot_general(ones, high, contract, preferred_element_type=jnp.float32)
-        norm += lax.dot_general(ones, low, contract, preferred_element_type=jnp.float32)
-        column_term = fold * norm[0:1, :]
-
-        @pl.loop(0, row_count // tile)
-        def _(step):
-            here = pl.ds(pl.multiple_of(step * tile, tile), tile)
-            inner = lax.dot_general(
-                rows_ref[here, :], points, contract, preferred_element_type=jnp.float32
-            )
-            exponent = (2.0 * fold) * inner + (row_term[here, :] - column_term)
-            kernel = jnp.exp2(exponent).astype(jnp.bfloat16)
-            out_ref[here, :] += jnp.dot(kernel, weights, preferred_element_type=jnp.float32)
-
-    waiting = [mine + sub for sub in range(SUBS)]
-
-    def add_oldest():
-        unit = waiting.pop(0)
-        transfer(unit, 1 - core, SIBLING).wait_recv()
-        add_unit(unit)
+        lanes = functools.reduce(
+            jnp.add, [squares[:, at:at + 128] for at in range(0, features, 128)]
+        )
+        column_term = fold * jnp.sum(lanes.T, axis=0, keepdims=True)
+        inner = lax.dot_general(
+            rows_ref[...], points, (((1,), (1,)), ((), ())), preferred_element_type=jnp.float32
+        )
+        exponent = (2.0 * fold) * inner + (row_term[...] - column_term)
+        kernel = jnp.exp2(exponent).astype(jnp.bfloat16)
+        out_ref[...] += jnp.dot(kernel, weights, preferred_element_type=jnp.float32)
 
     at_end, at_middle = arrivals(SUBS)
+    groups_of_end, groups_of_middle = complete_groups(at_end, group), complete_groups(at_middle, group)
+    for at in range(0, SUBS, group):
+        for sub in range(at, at + group):
+            transfer(mine + sub, 1 - core, SIBLING).wait_recv()
+        add_group(mine + at)
+
     passed = []
-    for end_entry, middle_entry in zip(at_end, at_middle, strict=True):
+    done = 0
+    for step, (end_entry, middle_entry) in enumerate(zip(at_end, at_middle, strict=True)):
         unit = jnp.where(is_end, unit_of(*end_entry[:4]), unit_of(*middle_entry[:4]))
         transfer(unit, core, SIBLING).wait_recv()
         for direction in (BESIDE, PARTNER, ACROSS, SIBLING):
@@ -260,16 +281,16 @@
                     transfer(unit, core, direction).start()
 
             passed.append((unit, direction, in_end, in_middle))
-        waiting.append(unit)
-        if len(waiting) > 1:
-            add_oldest()
-    while waiting:
-        add_oldest()
-
-    @pl.loop(0, row_count // tile)
-    def _(step):
-        here = pl.ds(pl.multiple_of(step * tile, tile), tile)
-        out_ref[here, :] = out_ref[here, :] / scale
+        last = step == len(at_end) - 1
+        while done < len(groups_of_end):
+            (end_step, *of_end), (middle_step, *of_middle) = groups_of_end[done], groups_of_middle[done]
+            if not last and max(end_step, middle_step) >= step:
+                break
+            first = jnp.where(is_end, unit_of(*of_end), unit_of(*of_middle))
+            for sub in range(group):
+                transfer(first + sub, 1 - core, SIBLING).wait_recv()
+            add_group(first)
+            done += 1
 
     for sub in range(SUBS):
         for direction in (PARTNER, BESIDE, SIBLING):
@@ -295,19 +316,23 @@
     devices = lax.axis_size("row") * lax.axis_size("col")
     columns = devices * shard
     units = devices // 2 * SUBS
-    return pl.pallas_call(
-        functools.partial(proof_kernel, float(columns)),
+    total = pl.pallas_call(
+        proof_kernel,
         out_shape=jax.ShapeDtypeStruct((rows, regimes), jnp.float32),
-        in_specs=[pl.BlockSpec(memory_space=pltpu.VMEM)] * 7,
+        in_specs=[pl.BlockSpec(memory_space=pltpu.HBM)] * 3
+        + [pl.BlockSpec(memory_space=pltpu.VMEM)] * 4,
         out_specs=pl.BlockSpec(memory_space=pltpu.VMEM),
         scratch_shapes=[
             pltpu.VMEM((columns, features + regimes), jnp.bfloat16),
+            pltpu.VMEM((rows, features), jnp.bfloat16),
+            pltpu.VMEM((shard, regimes), jnp.float32),
             pltpu.VMEM((rows, 1), jnp.float32),
+            pltpu.SemaphoreType.DMA((2 + SUBS,)),
             pltpu.SemaphoreType.DMA((units, 4)),
             pltpu.SemaphoreType.DMA((units * 2,)),
         ],
         compiler_params=pltpu.CompilerParams(
-            collective_id=0, has_side_effects=True, vmem_limit_bytes=40 * 2**20
+            collective_id=0, has_side_effects=True, vmem_limit_bytes=60 * 2**20
         ),
     )(
         row_points,
@@ -316,8 +341,9 @@
         behave_prob.reshape(1, shard),
         logged_action.reshape(1, shard),
         bucket.reshape(1, shard),
-        regime_table,
-    )
+        regime_table.T,
+    )
+    return total / float(columns)
 
 
 def solution(mesh):

time: 52.8 us -> 42.4 us (0.80)
  Pallas kernels: 47.7 us -> 40.2 us
  local copies, waits for them, and re-layouts: 4.77 us -> 0 us
  other arithmetic: 0 us -> 1.87 us
    pallas_call x1, Pallas kernels: 47.7 us -> 40.2 us  [relayed_body(): pl.pallas_call(proof_kernel, out_shape=jax.ShapeDtypeStruct((rows, regime...]
    unnamed x14 -> x0, local copies, waits for them, and re-layouts: 4.77 us -> none
    div x0 -> x1, other arithmetic: none -> 1.87 us  [relayed_body(): return total / float(columns)]
where the time goes in v2:
time: 42.4 us; the launch traced here: 42 us
  Pallas kernels  40.2 us (95%)
  other arithmetic  1.87 us (4%)
    pallas_call x1, Pallas kernels, relayed_body(): pl.pallas_call(proof_kernel, out_shape=jax.ShapeDtypeStruct((rows, regime...  40.2 us
    div x1, other arithmetic, relayed_body(): return total / float(columns)  1.87 us

profile of v2, /device:TPU:0, one launch (start us, length us, event | category | flops | bytes accessed | tf_op | source)
XLA Modules:
  0.0 42.0 jit_solution(2695297963415340313)
XLA Ops:
  0.0 40.2 %shard_map.73 = f32[1024,128]{1,0:T(8,128)} custom-call(bf16[1024,512]{1,0:T(8,128)(2,1)} %rows_hbm.1, bf16[256,512]{1,0:T(8,128)(2,1)} %next_hbm.1, f32[256,128]{1,0:T(8,128)} %ratio_hbm.1, f32[1,256]{1,0:T(1,128)} %bitcast.5, s32[1,256]{1,0:T(1,128)} %bitcast.6, s32[1,256]{1,0:T(1,128)} %bitcast.7, s32[64,128]{1,0:T(8,128)} %bitcast.4), custom_call_target="tpu_custom_call" | custom-call | tf_op jit(solution)/shard_map/pallas_call | solution.py:319
  40.2 1.9 %broadcast_multiply_fusion = f32[1024,128]{1,0:T(8,128)} fusion(f32[1024,128]{1,0:T(8,128)} %shard_map.73), kind=kLoop, calls=%fused_computation | loop fusion | flops 131072 | bytes 1048576 | tf_op jit(solution)/shard_map/div | solution.py:346

commit v3 on v2

--- a/solution.py
+++ b/solution.py
@@ -64,6 +64,7 @@
 
 
 SUBS = 4
+MIDDLE_BESIDE = 3
 PARTNER, ACROSS, BESIDE, SIBLING = range(4)
 
 
@@ -75,7 +76,7 @@
 
 
 def arrivals(subs):
-    half = subs // 2
+    half = MIDDLE_BESIDE
     every = list(range(subs))
 
     def block(other_column, end, other_side, parts, *directions):
@@ -95,7 +96,7 @@
     at_middle = interleaved(
         block(0, 0, 1, every, PARTNER, BESIDE) + block(0, 1, 1, every, PARTNER, BESIDE),
         block(0, 1, 0, every, ACROSS) + block(1, 1, 0, every),
-        block(1, 0, 0, every[half:], PARTNER)
+        block(1, 0, 0, every[half:])
         + block(1, 0, 0, every[:half])
         + block(1, 0, 1, every)
         + block(1, 1, 1, every),
@@ -216,19 +217,24 @@
         copy.wait()
     pl.semaphore_wait(barrier, jnp.where(is_end, 3, 4))
 
-    half = SUBS // 2
+    half = MIDDLE_BESIDE
+
+    @pl.when(is_end)
+    def _():
+        for sub in range(SUBS):
+            transfer(mine + sub, core, BESIDE).start()
+            transfer(mine + sub, core, PARTNER).start()
+
+    @pl.when(is_middle)
+    def _():
+        for sub in range(SUBS):
+            transfer(mine + sub, core, PARTNER).start()
+            transfer(mine + sub, core, ACROSS).start()
+        for sub in range(SUBS):
+            transfer(mine + (sub + half) % SUBS, core, BESIDE).start()
+
     for sub in range(SUBS):
-        for direction in (PARTNER, SIBLING):
-            transfer(mine + sub, core, direction).start()
-
-        @pl.when(is_end)
-        def _():
-            transfer(mine + sub, core, BESIDE).start()
-
-        @pl.when(is_middle)
-        def _():
-            transfer(mine + sub, core, ACROSS).start()
-            transfer(mine + (sub + half) % SUBS, core, BESIDE).start()
+        transfer(mine + sub, core, SIBLING).start()
 
     fold = KERNEL_SCALE / math.sqrt(features) * math.log2(math.e)
     rows_copy.wait()
@@ -260,17 +266,24 @@
 
     at_end, at_middle = arrivals(SUBS)
     groups_of_end, groups_of_middle = complete_groups(at_end, group), complete_groups(at_middle, group)
-    for at in range(0, SUBS, group):
-        for sub in range(at, at + group):
-            transfer(mine + sub, 1 - core, SIBLING).wait_recv()
-        add_group(mine + at)
+    waiting = [(1, mine + at) for at in range(0, SUBS, group)]
+    for (end_step, *of_end), (middle_step, *of_middle) in zip(
+        groups_of_end, groups_of_middle, strict=True
+    ):
+        first = jnp.where(is_end, unit_of(*of_end), unit_of(*of_middle))
+        waiting.append((max(end_step, middle_step) + 1, first))
+
+    def add_next():
+        _, first = waiting.pop(0)
+        for sub in range(group):
+            transfer(first + sub, 1 - core, SIBLING).wait_recv()
+        add_group(first)
 
     passed = []
-    done = 0
     for step, (end_entry, middle_entry) in enumerate(zip(at_end, at_middle, strict=True)):
         unit = jnp.where(is_end, unit_of(*end_entry[:4]), unit_of(*middle_entry[:4]))
         transfer(unit, core, SIBLING).wait_recv()
-        for direction in (BESIDE, PARTNER, ACROSS, SIBLING):
+        for direction in (PARTNER, ACROSS, BESIDE, SIBLING):
             in_end, in_middle = direction in end_entry[4], direction in middle_entry[4]
             if in_end and in_middle:
                 transfer(unit, core, direction).start()
@@ -281,16 +294,19 @@
                     transfer(unit, core, direction).start()
 
             passed.append((unit, direction, in_end, in_middle))
-        last = step == len(at_end) - 1
-        while done < len(groups_of_end):
-            (end_step, *of_end), (middle_step, *of_middle) = groups_of_end[done], groups_of_middle[done]
-            if not last and max(end_step, middle_step) >= step:
-                break
-            first = jnp.where(is_end, unit_of(*of_end), unit_of(*of_middle))
-            for sub in range(group):
-                transfer(first + sub, 1 - core, SIBLING).wait_recv()
-            add_group(first)
-            done += 1
+        if middle_entry[:4] == (0, 1, 1, SUBS - 1):
+            for sub in range(half, SUBS):
+                beside = unit_of(1, 0, 0, sub)
+
+                @pl.when(is_middle)
+                def _():
+                    transfer(beside, core, PARTNER).start()
+
+                passed.append((beside, PARTNER, False, True))
+        if waiting[0][0] <= step:
+            add_next()
+    while waiting:
+        add_next()
 
     for sub in range(SUBS):
         for direction in (PARTNER, BESIDE, SIBLING):

time: 42.4 us -> 38.5 us (0.908)
  Pallas kernels: 40.2 us -> 36.2 us
    pallas_call x1, Pallas kernels: 40.2 us -> 36.2 us  [relayed_body(): pl.pallas_call(proof_kernel, out_shape=jax.ShapeDtypeStruct((rows, regime...]
where the time goes in v3:
time: 38.5 us; the launch traced here: 38.1 us
  Pallas kernels  36.2 us (94%)
  other arithmetic  1.87 us (5%)
    pallas_call x1, Pallas kernels, relayed_body(): pl.pallas_call(proof_kernel, out_shape=jax.ShapeDtypeStruct((rows, regime...  36.2 us
    div x1, other arithmetic, relayed_body(): return total / float(columns)  1.87 us

profile of v3, /device:TPU:0, one launch (start us, length us, event | category | flops | bytes accessed | tf_op | source)
XLA Modules:
  0.0 38.1 jit_solution(4281458895865867518)
XLA Ops:
  0.0 36.2 %shard_map.73 = f32[1024,128]{1,0:T(8,128)} custom-call(bf16[1024,512]{1,0:T(8,128)(2,1)} %rows_hbm.1, bf16[256,512]{1,0:T(8,128)(2,1)} %next_hbm.1, f32[256,128]{1,0:T(8,128)} %ratio_hbm.1, f32[1,256]{1,0:T(1,128)} %bitcast.5, s32[1,256]{1,0:T(1,128)} %bitcast.6, s32[1,256]{1,0:T(1,128)} %bitcast.7, s32[64,128]{1,0:T(8,128)} %bitcast.4), custom_call_target="tpu_custom_call" | custom-call | tf_op jit(solution)/shard_map/pallas_call | solution.py:335
  36.2 1.9 %broadcast_multiply_fusion = f32[1024,128]{1,0:T(8,128)} fusion(f32[1024,128]{1,0:T(8,128)} %shard_map.73), kind=kLoop, calls=%fused_computation | loop fusion | flops 131072 | bytes 1048576 | tf_op jit(solution)/shard_map/div | solution.py:362

commit v4 on v3

--- a/solution.py
+++ b/solution.py
@@ -237,16 +237,18 @@
         transfer(mine + sub, core, SIBLING).start()
 
     fold = KERNEL_SCALE / math.sqrt(features) * math.log2(math.e)
-    rows_copy.wait()
     row_count = rows_ref.shape[0]
     tile = min(256, row_count)
 
-    @pl.loop(0, row_count // tile)
-    def _(step):
-        here = pl.ds(pl.multiple_of(step * tile, tile), tile)
-        squares = jnp.square(rows_ref[here, :].astype(jnp.float32))
-        row_term[here, :] = fold * (2.0 * features - jnp.sum(squares, axis=1, keepdims=True))
-        out_ref[here, :] = jnp.zeros((tile, out_ref.shape[1]), jnp.float32)
+    def prepare_rows():
+        rows_copy.wait()
+
+        @pl.loop(0, row_count // tile)
+        def _(step):
+            here = pl.ds(pl.multiple_of(step * tile, tile), tile)
+            squares = jnp.square(rows_ref[here, :].astype(jnp.float32))
+            row_term[here, :] = fold * (2.0 * features - jnp.sum(squares, axis=1, keepdims=True))
+            out_ref[here, :] = jnp.zeros((tile, out_ref.shape[1]), jnp.float32)
 
     def add_group(unit):
         start = pl.ds(pl.multiple_of(unit * 2 * sub_rows, width), width)
@@ -303,6 +305,8 @@
                     transfer(beside, core, PARTNER).start()
 
                 passed.append((beside, PARTNER, False, True))
+        if step == 1:
+            prepare_rows()
         if waiting[0][0] <= step:
             add_next()
     while waiting:

time: 38.5 us -> 38.5 us (level)
  no operation moved by 1% of the time
where the time goes in v4:
time: 38.5 us; the launch traced here: 38.1 us
  Pallas kernels  36.2 us (94%)
  other arithmetic  1.87 us (5%)
    pallas_call x1, Pallas kernels, relayed_body(): pl.pallas_call(proof_kernel, out_shape=jax.ShapeDtypeStruct((rows, regime...  36.2 us
    div x1, other arithmetic, relayed_body(): return total / float(columns)  1.87 us

profile of v4, /device:TPU:0, one launch (start us, length us, event | category | flops | bytes accessed | tf_op | source)
XLA Modules:
  0.0 38.1 jit_solution(11017963788899140082)
XLA Ops:
  0.0 36.2 %shard_map.73 = f32[1024,128]{1,0:T(8,128)} custom-call(bf16[1024,512]{1,0:T(8,128)(2,1)} %rows_hbm.1, bf16[256,512]{1,0:T(8,128)(2,1)} %next_hbm.1, f32[256,128]{1,0:T(8,128)} %ratio_hbm.1, f32[1,256]{1,0:T(1,128)} %bitcast.5, s32[1,256]{1,0:T(1,128)} %bitcast.6, s32[1,256]{1,0:T(1,128)} %bitcast.7, s32[64,128]{1,0:T(8,128)} %bitcast.4), custom_call_target="tpu_custom_call" | custom-call | tf_op jit(solution)/shard_map/pallas_call | solution.py:339
  36.3 1.9 %broadcast_multiply_fusion = f32[1024,128]{1,0:T(8,128)} fusion(f32[1024,128]{1,0:T(8,128)} %shard_map.73), kind=kLoop, calls=%fused_computation | loop fusion | flops 131072 | bytes 1048576 | tf_op jit(solution)/shard_map/div | solution.py:366
